TPU v7x, 128 devices: a whole 4x4x4 slice. The times are simulated.
128 devices in a mesh: row: 16 (over y, x_hi, core), col: 8 (over x_lo, z).
Axes of the slice: x: 4 (x_hi: 2, x_lo: 2; x = x_hi * 2 + x_lo), y: 4, z: 4, core: 2. Of those that a mesh axis runs over, the one named last changes fastest.
Arguments:
- inputs: bfloat16 [2048, 8192], P('row', 'col'), may hold values from -6 to 6
- cotangent: bfloat16 [2048, 8192], P('row', 'col'), may hold values from -6 to 6
- gate_pre: bfloat16 [2048, 14336], P('col', 'row'), may hold values from -8 to 8
- up_pre: bfloat16 [2048, 14336], P('col', 'row'), may hold values from -6 to 6
- w_gate: bfloat16 [8192, 14336], P('col', 'row'), may hold values from -0.0625 to 0.0625
- w_up: bfloat16 [8192, 14336], P('col', 'row'), may hold values from -0.0625 to 0.0625
- w_down: bfloat16 [14336, 8192], P('row', 'col'), may hold values from -0.046875 to 0.046875
Outputs:
- grad_inputs: bfloat16 [2048, 8192], P('row', 'col')
- grad_w_gate: bfloat16 [8192, 14336], P('col', 'row')
- grad_w_up: bfloat16 [8192, 14336], P('col', 'row')
- grad_w_down: bfloat16 [14336, 8192], P('row', 'col')
All inputs are finite; a program needn't handle non-finite values.
Results may differ from a plain program's by a relative error of at most 0.03.
Values may be sent and summed in bfloat16 or wider, within the bound.
A program may use at most 128 MiB of HBM per device.

v0:
```python
import jax
import jax.numpy as jnp
from jax import lax
from jax.sharding import PartitionSpec as P


def swiglu_back(gate_pre, up_pre, grad_hidden):
    gate = gate_pre.astype(jnp.float32)
    up = up_pre.astype(jnp.float32)
    sigma = jax.nn.sigmoid(gate)
    silu = gate * sigma
    hidden = (silu * up).astype(jnp.bfloat16)
    grad_gate = (grad_hidden * up * sigma * (1.0 + gate * (1.0 - sigma))).astype(jnp.bfloat16)
    grad_up = (grad_hidden * silu).astype(jnp.bfloat16)
    return (hidden, grad_gate, grad_up)


def shards(inputs, cotangent, gate_pre, up_pre, w_gate, w_up, w_down):
    across = (((1,), (1,)), ((), ()))
    along = (((0,), (0,)), ((), ()))
    cotangent_all = lax.all_gather(cotangent, "row", axis=0, tiled=True)
    grad_hidden = lax.psum_scatter(
        lax.dot_general(cotangent_all, w_down, across, preferred_element_type=jnp.float32).astype(
            jnp.bfloat16
        ),
        "col",
        scatter_dimension=0,
        tiled=True,
    ).astype(jnp.float32)
    hidden, grad_gate, grad_up = swiglu_back(gate_pre, up_pre, grad_hidden)
    hidden_all = lax.all_gather(hidden, "col", axis=0, tiled=True)
    gate_all, up_all = (
        lax.all_gather(grad_gate, "col", axis=0, tiled=True),
        lax.all_gather(grad_up, "col", axis=0, tiled=True),
    )
    grad_w_down = lax.dot_general(
        hidden_all, cotangent_all, along, preferred_element_type=jnp.float32
    ).astype(jnp.bfloat16)
    piece = lax.all_gather(inputs, "row", axis=0, tiled=True)
    gate_rows = gate_all
    up_rows = up_all
    gate_total = lax.dot_general(piece, gate_rows, along, preferred_element_type=jnp.float32)
    up_total = lax.dot_general(piece, up_rows, along, preferred_element_type=jnp.float32)
    gate_rows = gate_all
    up_rows = up_all
    total = lax.dot_general(gate_rows, w_gate, across, preferred_element_type=jnp.float32)
    grad_inputs = lax.psum_scatter(
        (total + lax.dot_general(up_rows, w_up, across, preferred_element_type=jnp.float32)).astype(
            jnp.bfloat16
        ),
        "row",
        scatter_dimension=0,
        tiled=True,
    )
    return (
        grad_inputs,
        gate_total.astype(jnp.bfloat16),
        up_total.astype(jnp.bfloat16),
        grad_w_down,
    )


def solution(mesh):
    placed = (
        P("row", "col"),
        P("row", "col"),
        P("col", "row"),
        P("col", "row"),
        P("col", "row"),
        P("col", "row"),
        P("row", "col"),
    )
    return jax.shard_map(
        shards,
        mesh=mesh,
        in_specs=placed,
        out_specs=(P("row", "col"), P("col", "row"), P("col", "row"), P("row", "col")),
        check_vma=False,
    )
```

profile of v0, /device:TPU:47, one launch (start us, length us, event | category | flops | bytes accessed | tf_op | source)
XLA Modules:
  0.0 414.4 jit_solution(14956954538691207557)
XLA Ops:
  7.2 0.0 copy-start
  7.2 0.0 all-gather.6.cloned.1.call-start
  7.2 0.7 all-gather.6.cloned.1.call-update
  7.9 0.0 reduce-scatter.3.cloned.1.call-start
  8.0 57.2 %all-gather.6.cloned.1.call-done = bf16[2048,1024]{1,0:T(8,128)(2,1)} async-done(((bf16[128,1024]{1,0:T(8,128)(2,1)}), bf16[2048,1024]{1,0:T(8,128)(2,1)}) %all-gather.6.cloned.1.call-update) | async-done | bytes 4194320 | tf_op jit(solution)/shard_map/all_gather | solution.py:21
  65.2 9.1 %convolution_convert_fusion = bf16[2048,896]{1,0:T(8,128)(2,1)} fusion(bf16[2048,1024]{1,0:T(8,128)(2,1)} %all-gather.6.cloned.1.call-done, bf16[896,1024]{1,0:T(8,128)(2,1)} %param.13), kind=kOutput, calls=%fused_computation.1 | convolution fusion | flops 3759931392 | bytes 9699328 | tf_op jit(solution)/shard_map/dot_general | solution.py:23
  74.3 0.0 reduce-scatter.3.cloned.1.call-update
  74.3 0.0 all-gather.8.cloned.1.call-start
  74.4 46.2 %reduce-scatter.3.cloned.1.call-done = bf16[256,896]{1,0:T(8,128)(2,1)} async-done(((bf16[2048,896]{1,0:T(8,128)(2,1)}), bf16[256,896]{1,0:T(8,128)(2,1)}) %reduce-scatter.3.cloned.1.call-update) | async-done | bytes 458768 | tf_op jit(solution)/shard_map/reduce_scatter | solution.py:22
  120.5 2.6 fusion.4
  123.1 0.0 all-gather.8.cloned.1.call-update
  123.2 0.0 all-gather.10.cloned.1.call-start
  123.2 0.5 all-gather.10.cloned.1.call-update
  123.7 0.0 all-gather.12.cloned.1.call-start
  123.8 0.5 all-gather.12.cloned.1.call-update
  124.3 0.0 all-gather.14.cloned.1.call-start
  124.4 0.5 all-gather.14.cloned.1.call-update
  124.9 0.2 reduce-scatter.5.cloned.1.call-start
  125.1 46.3 %all-gather.8.cloned.1.call-done = bf16[2048,896]{1,0:T(8,128)(2,1)} async-done(((bf16[256,896]{1,0:T(8,128)(2,1)}), bf16[2048,896]{1,0:T(8,128)(2,1)}) %all-gather.8.cloned.1.call-update) | async-done | bytes 3670032 | tf_op jit(solution)/shard_map/all_gather | solution.py:33
  171.4 0.0 copy-done
  171.4 8.9 %fusion.9 = f32[2048,1024]{1,0:T(8,128)} fusion(bf16[2048,896]{1,0:T(8,128)(2,1)} %all-gather.8.cloned.1.call-done, bf16[1024,896]{1,0:T(8,128)(2,1)S(1)} %copy-done), kind=kOutput, calls=%fused_computation.20 | convolution fusion | flops 3758096384 | bytes 13893632 | tf_op jit(solution)/shard_map/dot_general | solution.py:46
  180.3 40.2 %all-gather.10.cloned.1.call-done = bf16[2048,896]{1,0:T(8,128)(2,1)} async-done(((bf16[256,896]{1,0:T(8,128)(2,1)}), bf16[2048,896]{1,0:T(8,128)(2,1)}) %all-gather.10.cloned.1.call-update) | async-done | bytes 3670032 | tf_op jit(solution)/shard_map/all_gather | solution.py:34
  220.5 11.5 %add_convert_fusion = bf16[2048,1024]{1,0:T(8,128)(2,1)} fusion(f32[2048,1024]{1,0:T(8,128)} %fusion.9, bf16[2048,896]{1,0:T(8,128)(2,1)} %all-gather.10.cloned.1.call-done, bf16[1024,896]{1,0:T(8,128)(2,1)} %param.12), kind=kOutput, calls=%fused_computation | convolution fusion | flops 3762290688 | bytes 18087936 | tf_op jit(solution)/shard_map/dot_general | solution.py:48
  232.0 0.0 reduce-scatter.5.cloned.1.call-update
  232.1 45.1 %all-gather.12.cloned.1.call-done = bf16[2048,1024]{1,0:T(8,128)(2,1)} async-done(((bf16[128,1024]{1,0:T(8,128)(2,1)}), bf16[2048,1024]{1,0:T(8,128)(2,1)}) %all-gather.12.cloned.1.call-update) | async-done | bytes 4194320 | tf_op jit(solution)/shard_map/all_gather | solution.py:39
  277.2 8.5 %convert_bitcast_fusion.1 = bf16[1024,896]{0,1:T(8,128)(2,1)} fusion(bf16[2048,896]{1,0:T(8,128)(2,1)} %all-gather.8.cloned.1.call-done, bf16[2048,1024]{1,0:T(8,128)(2,1)} %all-gather.12.cloned.1.call-done), kind=kOutput, calls=%fused_computation.3 | convolution fusion | flops 3759013888 | bytes 9699328 | tf_op jit(solution)/shard_map/dot_general | solution.py:42
  285.7 3.8 copy.11
  289.5 8.6 %convert_bitcast_fusion = bf16[1024,896]{0,1:T(8,128)(2,1)} fusion(bf16[2048,896]{1,0:T(8,128)(2,1)} %all-gather.10.cloned.1.call-done, bf16[2048,1024]{1,0:T(8,128)(2,1)} %all-gather.12.cloned.1.call-done), kind=kOutput, calls=%fused_computation.2 | convolution fusion | flops 3759013888 | bytes 9699328 | tf_op jit(solution)/shard_map/dot_general | solution.py:43
  298.1 3.8 copy.12
  301.9 22.6 %all-gather.14.cloned.1.call-done = bf16[2048,896]{1,0:T(8,128)(2,1)} async-done(((bf16[256,896]{1,0:T(8,128)(2,1)}), bf16[2048,896]{1,0:T(8,128)(2,1)}) %all-gather.14.cloned.1.call-update) | async-done | bytes 3670032 | tf_op jit(solution)/shard_map/all_gather | solution.py:31
  324.5 8.5 %convolution_convert_fusion.1 = bf16[896,1024]{1,0:T(8,128)(2,1)} fusion(bf16[2048,896]{1,0:T(8,128)(2,1)} %all-gather.14.cloned.1.call-done, bf16[2048,1024]{1,0:T(8,128)(2,1)} %all-gather.6.cloned.1.call-done), kind=kOutput, calls=%fused_computation.4 | convolution fusion | flops 3759013888 | bytes 9699328 | tf_op jit(solution)/shard_map/dot_general | solution.py:36
  333.0 74.5 %reduce-scatter.5.cloned.1.call-done = bf16[128,1024]{1,0:T(8,128)(2,1)} async-done(((bf16[2048,1024]{1,0:T(8,128)(2,1)}), bf16[128,1024]{1,0:T(8,128)(2,1)}) %reduce-scatter.5.cloned.1.call-update) | async-done | bytes 262160 | tf_op jit(solution)/shard_map/reduce_scatter | solution.py:47
  (4 shorter events, 0.0 us)
Async XLA Ops:
  7.2 164.2 %copy-start = (bf16[1024,896]{1,0:T(8,128)(2,1)S(1)}, bf16[1024,896]{1,0:T(8,128)(2,1)}, u32[]{:S(2)}) copy-start(bf16[1024,896]{1,0:T(8,128)(2,1)} %param.11) | copy-start | bytes 5505028
  7.2 58.0 %all-gather.6.cloned.1.call-start = ((), (), s32[]{:S(2)}) async-start(), calls=%async_computation.2 | async-start | bytes 4456448 | tf_op jit(solution)/shard_map/all_gather | solution.py:21
  7.9 112.6 %reduce-scatter.3.cloned.1.call-start = ((), (), s32[]{:S(2)}) async-start(), calls=%async_computation.3 | async-start | bytes 4128768 | tf_op jit(solution)/shard_map/reduce_scatter | solution.py:22
  74.3 46.2 %copy-start.1 = (bf16[256,896]{1,0:T(8,128)(2,1)S(1)}, bf16[256,896]{1,0:T(8,128)(2,1)}, u32[]{:S(2)}) copy-start(bf16[256,896]{1,0:T(8,128)(2,1)} %param.10) | copy-start | bytes 1376260
  74.3 46.2 %copy-start.2 = (bf16[256,896]{1,0:T(8,128)(2,1)S(1)}, bf16[256,896]{1,0:T(8,128)(2,1)}, u32[]{:S(2)}) copy-start(bf16[256,896]{1,0:T(8,128)(2,1)} %param.9) | copy-start | bytes 1376260
  74.3 97.1 %all-gather.8.cloned.1.call-start = ((), (), s32[]{:S(2)}) async-start(), calls=%async_computation.4 | async-start | bytes 4128768 | tf_op jit(solution)/shard_map/all_gather | solution.py:33
  123.2 97.4 %all-gather.10.cloned.1.call-start = ((), (), s32[]{:S(2)}) async-start(), calls=%async_computation.5 | async-start | bytes 4128768 | tf_op jit(solution)/shard_map/all_gather | solution.py:34
  123.7 153.4 %all-gather.12.cloned.1.call-start = ((), (), s32[]{:S(2)}) async-start(), calls=%async_computation.7 | async-start | bytes 4456448 | tf_op jit(solution)/shard_map/all_gather | solution.py:39
  124.3 200.2 %all-gather.14.cloned.1.call-start = ((), (), s32[]{:S(2)}) async-start(), calls=%async_computation.8 | async-start | bytes 4128768 | tf_op jit(solution)/shard_map/all_gather | solution.py:31
  124.9 282.6 %reduce-scatter.5.cloned.1.call-start = ((), (), s32[]{:S(2)}) async-start(), calls=%async_computation.6 | async-start | bytes 4456448 | tf_op jit(solution)/shard_map/reduce_scatter | solution.py:47
Sparse Core Ops, SparseCore 0:
  10.5 54.6 all-gather.5
  74.4 46.0 reduce-scatter.2
  123.3 48.0 all-gather.7
  173.5 47.0 all-gather.9
  222.8 54.2 all-gather.11
  278.7 45.8 all-gather.13
  329.1 78.3 reduce-scatter.4
where the time goes:
time: 419 us; the launch traced here: 414 us
  waiting for transfers between devices  334 us (80%)
  matrix products  55.2 us (13%)
  between operations  14.1 us (3%)
  local copies, waits for them, and re-layouts  7.64 us (2%)
    reduce_scatter x1, waiting for transfers between devices, shards(): lax.psum_scatter((total + lax.dot_general(up_rows, w_up, across, preferre...  74.5 us
    all_gather x1, waiting for transfers between devices, shards(): cotangent_all = lax.all_gather(cotangent, 'row', axis=0, tiled=True)  57.2 us
    all_gather x1, waiting for transfers between devices, shards(): lax.all_gather(grad_gate, 'col', axis=0, tiled=True)  46.3 us
    reduce_scatter x1, waiting for transfers between devices, shards(): lax.psum_scatter(lax.dot_general(cotangent_all, w_down, across, preferred...  46.2 us
    all_gather x1, waiting for transfers between devices, shards(): piece = lax.all_gather(inputs, 'row', axis=0, tiled=True)  45.1 us
    all_gather x1, waiting for transfers between devices, shards(): lax.all_gather(grad_up, 'col', axis=0, tiled=True)  40.2 us
    all_gather x1, waiting for transfers between devices, shards(): hidden_all = lax.all_gather(hidden, 'col', axis=0, tiled=True)  22.6 us
    dot_general x1, matrix products, shards(): lax.dot_general(up_rows, w_up, across, preferred_element_type=jnp.float32)  11.5 us
  transfers between devices with their start and end apart: 7, of which 7 were waited for; matrix products, arithmetic and copies ran while one was open for 13% of the time, Pallas kernels for 0%

commit v1 on v0

v1 whole, which is shorter than its diff:
```python
import functools

import jax
import jax.numpy as jnp
from jax import lax
from jax.experimental import pallas as pl
from jax.experimental.pallas import tpu as pltpu
from jax.sharding import PartitionSpec as P

MESH = pl.DeviceIdType.MESH
BF16 = jnp.bfloat16
F32 = jnp.float32
ACROSS = (((1,), (1,)), ((), ()))

ROWS = 128
TOK = 256
HALF = 128
D = 1024
F = 896

N_ROWS = 17
N_HID = 8
N_GH = 14
N_G = 14
COT0 = 0
INP0 = COT0 + N_ROWS
HID0 = INP0 + N_ROWS
GH0 = HID0 + N_HID
G0 = GH0 + N_GH
PAIR0 = G0 + N_G
N_SEM = PAIR0 + 8


def kernel(
    inp_hbm, cot_hbm, gate_hbm, up_hbm, wg_hbm, wu_hbm, wd_hbm,
    gi_hbm, dwg_hbm, dwu_hbm, dwd_hbm,
    cot, inp_t, hid_t, grads, w_in, wd, inp_own, gate, up,
    slope, silu, gh_send, gh_recv, gh_keep, gh_own,
    gi_part, pair_send, pair_recv, q_send, q_recv,
    dw, dwd, gi_out,
    send_sem, recv_sem, q_send_sem, q_recv_sem, local_sem, out_sem,
):
    r = lax.axis_index("row")
    c = lax.axis_index("col")
    core = lax.rem(r, 2)
    chip = lax.div(r, 2)
    xh = lax.rem(chip, 2)
    y = lax.div(chip, 2)
    xl = lax.div(c, 4)
    z = lax.rem(c, 4)

    def row_of(y_, xh_, core_):
        return (y_ * 2 + xh_) * 2 + core_

    y_up, y_dn, y_far = lax.rem(y + 1, 4), lax.rem(y + 3, 4), lax.rem(y + 2, 4)
    z_up, z_dn, z_far = lax.rem(z + 1, 4), lax.rem(z + 3, 4), lax.rem(z + 2, 4)
    xo = 1 - xl
    xho = 1 - xh
    c_xl = xo * 4 + z

    to_yp = (row_of(y_up, xh, core), c)
    to_ym = (row_of(y_dn, xh, core), c)
    to_xh = (row_of(y, xho, core), c)
    to_core = (row_of(y, xh, 1 - core), c)
    to_zp = (r, xl * 4 + z_up)
    to_zm = (r, xl * 4 + z_dn)
    to_xl = (r, c_xl)

    def local(i, src, dst):
        return pltpu.make_async_copy(src, dst, local_sem.at[i])

    def tile(start, size, step):
        return pl.ds(pl.multiple_of(start, step), size)

    def rows(r_):
        return tile(r_ * ROWS, ROWS, ROWS)

    def toks(c_):
        return tile(c_ * TOK, TOK, TOK)

    def halves(c_, h):
        return tile(c_ * TOK + h * HALF, HALF, HALF)

    loads = [
        local(0, cot_hbm, cot.at[rows(r), :]),
        local(1, gate_hbm, gate),
        local(2, up_hbm, up),
        local(3, inp_hbm, inp_own),
        local(4, wd_hbm, wd),
        local(5, wg_hbm, w_in.at[:, pl.ds(0, F)]),
        local(6, wu_hbm, w_in.at[:, pl.ds(F, F)]),
    ]
    for load in loads:
        load.start()

    barrier = pltpu.get_barrier_semaphore()
    partners = [to_yp, to_ym, to_xh, to_core, to_zp, to_zm, to_xl]
    for device in partners:
        pl.semaphore_signal(barrier, inc=1, device_id=device, device_id_type=MESH)
    far = [
        (row_of(y_far, xh, core), c),
        (row_of(y_up, xho, core), c),
        (row_of(y_dn, xho, core), c),
        (row_of(y_far, xho, core), c),
    ]
    for device in far:
        pl.semaphore_signal(barrier, inc=1, device_id=device, device_id_type=MESH)
    pl.semaphore_wait(barrier, len(partners) + len(far))

    started = []

    def message(i, src, dst, device):
        return pltpu.make_async_remote_copy(
            src_ref=src,
            dst_ref=dst,
            send_sem=send_sem.at[i],
            recv_sem=recv_sem.at[i],
            device_id=device,
            device_id_type=MESH,
        )

    def send(m):
        m.start()
        started.append(m)

    def row_gather(base, at):
        m = {}

        def add(name, i, y_, xh_, part, device):
            ref = at(y_, xh_, part)
            m[name] = message(base + i, ref, ref, device)

        add("own>xh", 0, y, xh, None, to_xh)
        add("own>y+", 1, y, xh, None, to_yp)
        add("own>y-", 2, y, xh, None, to_ym)
        add("xh>y+", 3, y, xho, None, to_yp)
        add("xh>y-", 4, y, xho, None, to_ym)
        add("own2>y+", 5, y_dn, xh, 0, to_yp)
        add("own2>y-", 6, y_up, xh, 1, to_ym)
        add("xh2>y+", 7, y_dn, xho, 0, to_yp)
        add("xh2>y-", 8, y_up, xho, 1, to_ym)
        k = 9
        for yn, y_ in (("0", y), ("-", y_dn), ("+", y_up), ("f", y_far)):
            for xn, xh_ in (("own", xh), ("xh", xho)):
                add(xn + yn + ">core", k, y_, xh_, None, to_core)
                k += 1
        return m

    def cot_at(y_, xh_, part):
        start = row_of(y_, xh_, core) * ROWS
        if part is None:
            return cot.at[tile(start, ROWS, ROWS), :]
        return cot.at[tile(start + part * (ROWS // 2), ROWS // 2, ROWS // 2), :]

    def inp_at(y_, xh_, part):
        cols = tile(row_of(y_, xh_, core) * ROWS, ROWS, ROWS)
        if part is None:
            return inp_t.at[:, cols]
        return inp_t.at[pl.ds(part * (D // 2), D // 2), cols]

    cm = row_gather(COT0, cot_at)
    im = row_gather(INP0, inp_at)

    def row_start(m):
        send(m["own>xh"])
        send(m["own>y+"])
        send(m["own>y-"])
        send(m["own0>core"])

    def row_xh(m):
        m["own>xh"].wait_recv()
        send(m["xh>y+"])
        send(m["xh>y-"])
        send(m["xh0>core"])

    def row_near(m, which):
        m[which + ">y+"].wait_recv()
        send(m[which + "2>y+"])
        send(m[which + "->core"])
        m[which + ">y-"].wait_recv()
        send(m[which + "2>y-"])
        send(m[which + "+>core"])

    def row_far(m, which):
        m[which + "2>y+"].wait_recv()
        m[which + "2>y-"].wait_recv()
        send(m[which + "f>core"])

    def row_finish(m):
        for name in m:
            if name.endswith(">core"):
                m[name].wait_recv()

    loads[0].wait()
    row_start(cm)
    loads[1].wait()
    loads[2].wait()

    def activate(t, _):
        part = pl.ds(pl.multiple_of(t * 16, 16), 16)
        g = gate[part, :].astype(F32)
        u = up[part, :].astype(F32)
        s = 1.0 / (1.0 + jnp.exp(-g))
        sl = g * s
        silu[part, :] = sl
        slope[part, :] = u * s * (1.0 + g * (1.0 - s))
        gh_own[part, :] = sl * u
        return 0

    lax.fori_loop(0, TOK // 16, activate, 0)

    def turn(t, _):
        part = pl.ds(pl.multiple_of(t * 128, 128), 128)
        hid_t[part, toks(c)] = gh_own[:, part].T.astype(BF16)
        return 0

    lax.fori_loop(0, F // 128, turn, 0)

    def hid_at(c_, part):
        if part is None:
            return hid_t.at[:, toks(c_)]
        return hid_t.at[pl.ds(part * (F // 2), F // 2), toks(c_)]

    hm = {}

    def hid_add(name, i, c_, part, device):
        ref = hid_at(c_, part)
        hm[name] = message(HID0 + i, ref, ref, device)

    c_zp, c_zm, c_zf = xl * 4 + z_up, xl * 4 + z_dn, xl * 4 + z_far
    hid_add("own>z+", 0, c, None, to_zp)
    hid_add("own>z-", 1, c, None, to_zm)
    hid_add("own>xl", 2, c, None, to_xl)
    hid_add("far>z+", 3, c_zm, 0, to_zp)
    hid_add("far>z-", 4, c_zp, 1, to_zm)
    hid_add("zm>xl", 5, c_zm, None, to_xl)
    hid_add("zp>xl", 6, c_zp, None, to_xl)
    hid_add("zf>xl", 7, c_zf, None, to_xl)
    send(hm["own>z+"])
    send(hm["own>z-"])
    send(hm["own>xl"])

    loads[3].wait()

    def turn_inp(t, _):
        part = pl.ds(pl.multiple_of(t * 128, 128), 128)
        inp_t[part, rows(r)] = inp_own[:, part].astype(F32).T.astype(BF16)
        return 0

    lax.fori_loop(0, D // 128, turn_inp, 0)

    row_xh(cm)
    row_near(cm, "own")
    hm["own>z+"].wait_recv()
    send(hm["far>z+"])
    send(hm["zm>xl"])
    hm["own>z-"].wait_recv()
    send(hm["far>z-"])
    send(hm["zp>xl"])
    row_near(cm, "xh")
    row_start(im)
    row_far(cm, "own")
    row_far(cm, "xh")
    hm["far>z+"].wait_recv()
    hm["far>z-"].wait_recv()
    send(hm["zf>xl"])
    row_finish(cm)
    loads[4].wait()

    def gh_dot(c_):
        return lax.dot_general(cot[toks(c_), :], wd[...], ACROSS, preferred_element_type=F32)

    gm = {}

    def gh_add(name, i, device):
        gm[name] = message(GH0 + i, gh_send.at[i], gh_recv.at[i], device)

    for k, who in enumerate(("other", "own")):
        gh_add("relay+" + who, 0 + k, to_zp)
        gh_add("relay-" + who, 2 + k, to_zm)
        gh_add("direct+" + who, 4 + k, to_zp)
        gh_add("direct-" + who, 6 + k, to_zm)
        gh_add("comb+" + who, 8 + k, to_zp)
        gh_add("comb-" + who, 10 + k, to_zm)
        gh_add("xl%d" % k, 12 + k, to_xl)
    sides = (("other", 0, xo), ("own", 1, xl))

    for who, k, x_ in sides:
        part = gh_dot(x_ * 4 + z_far).astype(BF16)
        gh_send[0 + k] = part[:HALF]
        gh_send[2 + k] = part[HALF:]
        send(gm["relay+" + who])
        send(gm["relay-" + who])
    for who, k, x_ in sides:
        part = gh_dot(x_ * 4 + z_up)
        gh_send[4 + k] = part[HALF:].astype(BF16)
        gh_keep[k] = part[:HALF]
        send(gm["direct+" + who])
        part = gh_dot(x_ * 4 + z_dn)
        gh_send[6 + k] = part[:HALF].astype(BF16)
        gh_keep[2 + k] = part[HALF:]
        send(gm["direct-" + who])
    gh_own[...] = gh_dot(xo * 4 + z)
    row_xh(im)
    for who, k, x_ in sides:
        gm["relay+" + who].wait_recv()
        gh_send[8 + k] = (gh_keep[k] + gh_recv[0 + k].astype(F32)).astype(BF16)
        send(gm["comb+" + who])
        gm["relay-" + who].wait_recv()
        gh_send[10 + k] = (gh_keep[2 + k] + gh_recv[2 + k].astype(F32)).astype(BF16)
        send(gm["comb-" + who])
    row_near(im, "own")
    row_near(im, "xh")
    gm["direct+other"].wait_recv()
    gm["direct-other"].wait_recv()
    gm["comb+other"].wait_recv()
    gm["comb-other"].wait_recv()
    gh_send[12] = (
        gh_own[pl.ds(0, HALF), :] + gh_recv[6].astype(F32) + gh_recv[8].astype(F32)
    ).astype(BF16)
    send(gm["xl0"])
    gh_send[13] = (
        gh_own[pl.ds(HALF, HALF), :] + gh_recv[4].astype(F32) + gh_recv[10].astype(F32)
    ).astype(BF16)
    send(gm["xl1"])
    gh_own[...] = gh_dot(c)
    row_far(im, "own")
    row_far(im, "xh")
    gm["direct+own"].wait_recv()
    gm["direct-own"].wait_recv()
    gm["comb+own"].wait_recv()
    gm["comb-own"].wait_recv()

    gg = {}

    def g_add(name, i, c_, h, device):
        ref = grads.at[halves(c_, h), :]
        gg[name] = message(G0 + i, ref, ref, device)

    c_xzp, c_xzm, c_xzf = xo * 4 + z_up, xo * 4 + z_dn, xo * 4 + z_far
    for h in (0, 1):
        g_add("own%d>z+" % h, 0 + h, c, h, to_zp)
        g_add("own%d>z-" % h, 2 + h, c, h, to_zm)
        g_add("own%d>xl" % h, 4 + h, c, h, to_xl)
        g_add("xl%d>z+" % h, 6 + h, c_xl, h, to_zp)
        g_add("xl%d>z-" % h, 8 + h, c_xl, h, to_zm)
    g_add("far>z+", 10, c_zm, 0, to_zp)
    g_add("far>z-", 11, c_zp, 1, to_zm)
    g_add("xfar>z+", 12, c_xzm, 0, to_zp)
    g_add("xfar>z-", 13, c_xzp, 1, to_zm)

    for h in (0, 1):
        gm["xl%d" % h].wait_recv()
        a, b = ((6, 8), (4, 10))[h]

        def grad(t, _, h=h, a=a, b=b):
            here = pl.ds(pl.multiple_of(t * 16, 16), 16)
            part = pl.ds(pl.multiple_of(h * HALF + t * 16, 16), 16)
            gh = (
                gh_own[part, :]
                + gh_recv[a + 1, here, :].astype(F32)
                + gh_recv[b + 1, here, :].astype(F32)
                + gh_recv[12 + h, here, :].astype(F32)
            )
            dst = tile(c * TOK + h * HALF + t * 16, 16, 16)
            grads[dst, pl.ds(0, F)] = (gh * slope[part, :]).astype(BF16)
            grads[dst, pl.ds(F, F)] = (gh * silu[part, :]).astype(BF16)
            return 0

        lax.fori_loop(0, HALF // 16, grad, 0)
        send(gg["own%d>z+" % h])
        send(gg["own%d>z-" % h])
        send(gg["own%d>xl" % h])

    loads[5].wait()
    loads[6].wait()

    pairs = []
    sums = []

    def gi_make(c_):
        i = len(pairs)
        gi_part[i % 2] = lax.dot_general(
            grads[toks(c_), :], w_in[...], ACROSS, preferred_element_type=F32
        )
        theirs = tile((1 - core) * ROWS, ROWS, ROWS)
        pair_send[i] = gi_part[i % 2, theirs, :].astype(BF16)
        m = message(PAIR0 + i, pair_send.at[i], pair_recv.at[i], to_core)
        send(m)
        pairs.append((m, c_))

    def gi_sum():
        i = len(sums)
        m, c_ = pairs[i]
        m.wait_recv()
        mine = tile(core * ROWS, ROWS, ROWS)
        total = (gi_part[i % 2, mine, :] + pair_recv[i].astype(F32)).astype(BF16)
        q_send[i] = total
        q = pltpu.make_async_remote_copy(
            src_ref=q_send.at[i],
            dst_ref=q_recv.at[chip],
            send_sem=q_send_sem.at[i],
            recv_sem=q_recv_sem.at[chip],
            device_id=(c_ * 2 + core, c),
            device_id_type=MESH,
        )
        here = c_ == chip

        @pl.when(jnp.logical_not(here))
        def _():
            q.start()

        @pl.when(here)
        def _():
            q_recv[chip] = q_send[i]

        sums.append((q, here))

    gi_make(c)

    row_finish(im)
    for name in ("own>xl", "zm>xl", "zp>xl", "zf>xl"):
        hm[name].wait_recv()

    gg["own0>xl"].wait_recv()
    send(gg["xl0>z+"])
    send(gg["xl0>z-"])
    gg["own0>z+"].wait_recv()
    send(gg["far>z+"])
    gg["own0>z-"].wait_recv()

    def down(t, _):
        part = pl.ds(pl.multiple_of(t * 224, 32), 224)
        dwd[part, :] = jnp.dot(
            hid_t[part, :], cot[...], preferred_element_type=F32
        ).astype(BF16)
        return 0

    lax.fori_loop(0, 4, down, 0)
    outs = [pltpu.make_async_copy(dwd, dwd_hbm, out_sem.at[0])]
    outs[0].start()

    gg["own1>xl"].wait_recv()
    send(gg["xl1>z+"])
    send(gg["xl1>z-"])
    gi_make(c_xl)
    gi_sum()
    gg["own1>z-"].wait_recv()
    send(gg["far>z-"])
    gg["own1>z+"].wait_recv()
    gi_make(c_zm)
    gi_sum()
    gi_make(c_zp)
    gi_sum()
    gg["xl0>z+"].wait_recv()
    send(gg["xfar>z+"])
    gg["xl0>z-"].wait_recv()
    gg["xl1>z-"].wait_recv()
    send(gg["xfar>z-"])
    gg["xl1>z+"].wait_recv()
    gi_make(c_xzm)
    gi_sum()
    gi_make(c_xzp)
    gi_sum()
    gg["far>z+"].wait_recv()
    gg["far>z-"].wait_recv()
    gi_make(c_zf)
    gi_sum()
    gg["xfar>z+"].wait_recv()
    gg["xfar>z-"].wait_recv()
    gi_make(c_xzf)
    gi_sum()
    gi_sum()

    for k, dst in ((0, dwg_hbm), (1, dwu_hbm)):

        def inward(t, _, k=k):
            part = pl.ds(pl.multiple_of(t * 256, 256), 256)
            dw[k, part, :] = jnp.dot(
                inp_t[part, :], grads[:, pl.ds(k * F, F)], preferred_element_type=F32
            ).astype(BF16)
            return 0

        lax.fori_loop(0, 4, inward, 0)
        copy = pltpu.make_async_copy(dw.at[k], dst, out_sem.at[1 + k])
        copy.start()
        outs.append(copy)

    for j in range(8):
        arrival = pltpu.make_async_remote_copy(
            src_ref=q_send.at[j],
            dst_ref=q_recv.at[j],
            send_sem=q_send_sem.at[j],
            recv_sem=q_recv_sem.at[j],
            device_id=to_core,
            device_id_type=MESH,
        )

        @pl.when(chip != j)
        def _():
            arrival.wait_recv()

    def finish(t, _):
        part = pl.ds(pl.multiple_of(t * 16, 16), 16)
        total = q_recv[0, part, :].astype(F32)
        for j in range(1, 8):
            total = total + q_recv[j, part, :].astype(F32)
        gi_out[part, :] = total.astype(BF16)
        return 0

    lax.fori_loop(0, ROWS // 16, finish, 0)
    copy = pltpu.make_async_copy(gi_out, gi_hbm, out_sem.at[3])
    copy.start()
    outs.append(copy)
    for m in started:
        m.wait_send()
    for q, here in sums:

        @pl.when(jnp.logical_not(here))
        def _():
            q.wait_send()

    for copy in outs:
        copy.wait()


def shards(inputs, cotangent, gate_pre, up_pre, w_gate, w_up, w_down):
    anywhere = pl.BlockSpec(memory_space=pl.ANY)
    vmem = pltpu.VMEM
    dma = pltpu.SemaphoreType.DMA
    return pl.pallas_call(
        kernel,
        out_shape=(
            jax.ShapeDtypeStruct((ROWS, D), BF16),
            jax.ShapeDtypeStruct((D, F), BF16),
            jax.ShapeDtypeStruct((D, F), BF16),
            jax.ShapeDtypeStruct((F, D), BF16),
        ),
        in_specs=[anywhere] * 7,
        out_specs=(anywhere,) * 4,
        scratch_shapes=[
            vmem((2048, D), BF16),
            vmem((D, 2048), BF16),
            vmem((F, 2048), BF16),
            vmem((2048, 2 * F), BF16),
            vmem((D, 2 * F), BF16),
            vmem((F, D), BF16),
            vmem((ROWS, D), BF16),
            vmem((TOK, F), BF16),
            vmem((TOK, F), BF16),
            vmem((TOK, F), F32),
            vmem((TOK, F), F32),
            vmem((14, HALF, F), BF16),
            vmem((14, HALF, F), BF16),
            vmem((4, HALF, F), F32),
            vmem((TOK, F), F32),
            vmem((2, TOK, D), F32),
            vmem((8, ROWS, D), BF16),
            vmem((8, ROWS, D), BF16),
            vmem((8, ROWS, D), BF16),
            vmem((8, ROWS, D), BF16),
            vmem((2, D, F), BF16),
            vmem((F, D), BF16),
            vmem((ROWS, D), BF16),
            dma((N_SEM,)),
            dma((N_SEM,)),
            dma((8,)),
            dma((8,)),
            dma((7,)),
            dma((4,)),
        ],
        compiler_params=pltpu.CompilerParams(
            collective_id=0, has_side_effects=True, vmem_limit_bytes=60 * 2**20
        ),
    )(inputs, cotangent, gate_pre, up_pre, w_gate, w_up, w_down)


def solution(mesh):
    placed = (
        P("row", "col"),
        P("row", "col"),
        P("col", "row"),
        P("col", "row"),
        P("col", "row"),
        P("col", "row"),
        P("row", "col"),
    )
    return jax.shard_map(
        shards,
        mesh=mesh,
        in_specs=placed,
        out_specs=(P("row", "col"), P("col", "row"), P("col", "row"), P("row", "col")),
        check_vma=False,
    )
```

time: 419 us -> 162 us (0.39)
  waiting for transfers between devices: 334 us -> 0 us
  Pallas kernels: 0 us -> 151 us
  matrix products: 55.2 us -> 0 us
  between operations: 14.1 us -> 0.65 us
    all_gather x5 -> x0, waiting for transfers between devices: 211 us -> none  [the longest x1 57.2 us: shards(): cotangent_all = lax.all_gather(cotangent, 'row', axis=0, tiled=True)]
    pallas_call x0 -> x1, Pallas kernels: none -> 151 us  [shards(): pl.pallas_call(kernel, out_shape=(jax.ShapeDtypeStruct((ROWS, D), BF16),...]
    reduce_scatter x2 -> x0, waiting for transfers between devices: 121 us -> none  [the longest x1 74.5 us: shards(): lax.psum_scatter((total + lax.dot_general(up_rows, w_up, across, preferre...]
    dot_general x6 -> x0, matrix products: 55.2 us -> none  [the longest x1 11.5 us: shards(): lax.dot_general(up_rows, w_up, across, preferred_element_type=jnp.float32)]
  transfers between devices with their start and end apart: 7 -> 0, of which waited for: 7 -> 0; matrix products, arithmetic and copies ran while one was open for 13% -> 0% of each run, Pallas kernels for 0% -> 0%
where the time goes in v1:
time: 162 us; the launch traced here: 160 us
  Pallas kernels  151 us (93%)
  local copies, waits for them, and re-layouts  8.07 us (5%)
    pallas_call x1, Pallas kernels, shards(): pl.pallas_call(kernel, out_shape=(jax.ShapeDtypeStruct((ROWS, D), BF16),...  151 us
    unnamed x8, local copies, waits for them, and re-layouts  8.07 us

profile of v1, /device:TPU:47, one launch (start us, length us, event | category | flops | bytes accessed | tf_op | source)
XLA Modules:
  0.0 159.6 jit_solution(8330183447928936974)
XLA Ops:
  0.6 150.9 %shard_map.102 = (bf16[128,1024]{1,0:T(8,128)(2,1)}, bf16[1024,896]{1,0:T(8,128)(2,1)}, bf16[1024,896]{1,0:T(8,128)(2,1)}, bf16[896,1024]{1,0:T(8,128)(2,1)}) custom-call(bf16[128,1024]{1,0:T(8,128)(2,1)} %inp_hbm.1, bf16[128,1024]{1,0:T(8,128)(2,1)} %cot_hbm.1, bf16[256,896]{1,0:T(8,128)(2,1)} %gate_hbm.1, bf16[256,896]{1,0:T(8,128)(2,1)} %up_hbm.1, ...), custom_call_target="tpu_custom_call" | custom-call | tf_op jit(solution)/shard_map/pallas_call | solution.py:531
  151.5 1.7 %copy.15 = bf16[128,1024]{1,0:T(8,128)(2,1)} copy(bf16[128,1024]{1,0:T(8,128)(2,1)} %get-tuple-element.8) | data formatting | bytes 524288
  153.2 0.0 copy-start.1
  153.2 3.0 %copy.16 = bf16[1024,896]{1,0:T(8,128)(2,1)} copy(bf16[1024,896]{1,0:T(8,128)(2,1)} %get-tuple-element.9) | data formatting | bytes 3670016
  156.2 0.0 copy-done.1
  156.2 0.0 copy-start
  156.2 1.2 copy.17
  157.5 0.9 copy-done
  158.4 1.2 copy.18
Async XLA Ops:
  153.2 3.0 %copy-start.1 = (bf16[1024,896]{1,0:T(8,128)(2,1)S(1)}, bf16[1024,896]{1,0:T(8,128)(2,1)}, u32[]{:S(2)}) copy-start(bf16[1024,896]{1,0:T(8,128)(2,1)} %get-tuple-element.10) | copy-start | bytes 5505028
  156.2 2.2 %copy-start = (bf16[896,1024]{1,0:T(8,128)(2,1)S(1)}, bf16[896,1024]{1,0:T(8,128)(2,1)}, u32[]{:S(2)}) copy-start(bf16[896,1024]{1,0:T(8,128)(2,1)} %get-tuple-element.11) | copy-start | bytes 5505028

commit v2 on v1

v2 whole, which is shorter than its diff:
```python
import functools

import jax
import jax.numpy as jnp
from jax import lax
from jax.experimental import pallas as pl
from jax.experimental.pallas import tpu as pltpu
from jax.sharding import PartitionSpec as P

MESH = pl.DeviceIdType.MESH
BF16 = jnp.bfloat16
F32 = jnp.float32
ACROSS = (((1,), (1,)), ((), ()))

ROWS = 128
TOK = 256
HALF = 128
FWD = 48
LATE = 32
D = 1024
F = 896

N_ROWS = 17
N_HID = 17
N_GH = 14
N_G = 30
COT0 = 0
INP0 = COT0 + N_ROWS
HID0 = INP0 + N_ROWS
GH0 = HID0 + N_HID
G0 = GH0 + N_GH
PAIR0 = G0 + N_G
N_FWD = 3
FWD0 = PAIR0 + 9
N_SEM = FWD0 + N_FWD
PARTS = 4


def kernel(
    inp_hbm, cot_hbm, gate_hbm, up_hbm, wg_hbm, wu_hbm, wd_hbm,
    gi_hbm, dwg_hbm, dwu_hbm, dwd_hbm,
    cot, inp_t, hid_t, grads, w_in, wd, inp_own, gate, up,
    slope, silu, gh_send, gh_recv, gh_keep, gh_own,
    gi_part, pair_send, pair_recv, q_send, q_recv, x_send, x_recv,
    dw, dw_sum, dwd, gi_out,
    send_sem, recv_sem, q_send_sem, q_recv_sem, q_late_sem, local_sem, out_sem,
):
    r = lax.axis_index("row")
    c = lax.axis_index("col")
    core = lax.rem(r, 2)
    chip = lax.div(r, 2)
    xh = lax.rem(chip, 2)
    y = lax.div(chip, 2)
    xl = lax.div(c, 4)
    z = lax.rem(c, 4)

    def row_of(y_, xh_, core_):
        return (y_ * 2 + xh_) * 2 + core_

    y_up, y_dn, y_far = lax.rem(y + 1, 4), lax.rem(y + 3, 4), lax.rem(y + 2, 4)
    z_up, z_dn, z_far = lax.rem(z + 1, 4), lax.rem(z + 3, 4), lax.rem(z + 2, 4)
    xo = 1 - xl
    xho = 1 - xh
    c_xl = xo * 4 + z

    to_yp = (row_of(y_up, xh, core), c)
    to_ym = (row_of(y_dn, xh, core), c)
    to_xh = (row_of(y, xho, core), c)
    to_core = (row_of(y, xh, 1 - core), c)
    to_zp = (r, xl * 4 + z_up)
    to_zm = (r, xl * 4 + z_dn)
    to_xl = (r, c_xl)

    def local(i, src, dst):
        return pltpu.make_async_copy(src, dst, local_sem.at[i])

    def tile(start, size, step):
        return pl.ds(pl.multiple_of(start, step), size)

    def rows(r_):
        return tile(r_ * ROWS, ROWS, ROWS)

    def toks(c_):
        return tile(c_ * TOK, TOK, TOK)

    def halves(c_, h):
        return tile(c_ * TOK + h * HALF, HALF, HALF)

    loads = [
        local(0, cot_hbm, cot.at[rows(r), :]),
        local(1, gate_hbm, gate),
        local(2, up_hbm, up),
        local(3, inp_hbm, inp_own),
        local(4, wd_hbm, wd),
        local(5, wg_hbm, w_in.at[:, pl.ds(0, F)]),
        local(6, wu_hbm, w_in.at[:, pl.ds(F, F)]),
    ]
    for load in loads:
        load.start()

    barrier = pltpu.get_barrier_semaphore()
    partners = [to_yp, to_ym, to_xh, to_core, to_zp, to_zm, to_xl]
    for device in partners:
        pl.semaphore_signal(barrier, inc=1, device_id=device, device_id_type=MESH)
    far = [
        (row_of(y_far, xh, core), c),
        (row_of(y_up, xho, core), c),
        (row_of(y_dn, xho, core), c),
        (row_of(y_far, xho, core), c),
    ]
    for device in far:
        pl.semaphore_signal(barrier, inc=1, device_id=device, device_id_type=MESH)
    pl.semaphore_wait(barrier, len(partners) + len(far))

    started = []

    def message(i, src, dst, device):
        return pltpu.make_async_remote_copy(
            src_ref=src,
            dst_ref=dst,
            send_sem=send_sem.at[i],
            recv_sem=recv_sem.at[i],
            device_id=device,
            device_id_type=MESH,
        )

    def send(m):
        m.start()
        started.append(m)

    def row_gather(base, at):
        m = {}

        def add(name, i, y_, xh_, part, device):
            ref = at(y_, xh_, part)
            m[name] = message(base + i, ref, ref, device)

        add("oh", 0, y, xh, None, to_xh)
        add("oy+", 1, y, xh, None, to_yp)
        add("oy-", 2, y, xh, None, to_ym)
        add("hy+", 3, y, xho, None, to_yp)
        add("hy-", 4, y, xho, None, to_ym)
        add("o2y+", 5, y_dn, xh, 0, to_yp)
        add("o2y-", 6, y_up, xh, 1, to_ym)
        add("h2y+", 7, y_dn, xho, 0, to_yp)
        add("h2y-", 8, y_up, xho, 1, to_ym)
        k = 9
        for yn, y_ in (("0", y), ("-", y_dn), ("+", y_up), ("f", y_far)):
            for xn, xh_ in (("o", xh), ("h", xho)):
                add(xn + yn + "c", k, y_, xh_, None, to_core)
                k += 1
        return m

    def cot_at(y_, xh_, part):
        start = row_of(y_, xh_, core) * ROWS
        if part is None:
            return cot.at[tile(start, ROWS, ROWS), :]
        return cot.at[tile(start + part * (ROWS // 2), ROWS // 2, ROWS // 2), :]

    def inp_at(y_, xh_, part):
        cols = tile(row_of(y_, xh_, core) * ROWS, ROWS, ROWS)
        if part is None:
            return inp_t.at[:, cols]
        return inp_t.at[pl.ds(part * (D // 2), D // 2), cols]

    cm = row_gather(COT0, cot_at)
    im = row_gather(INP0, inp_at)

    def row_start(m):
        send(m["oh"])
        send(m["oy+"])
        send(m["oy-"])
        send(m["o0c"])

    def row_xh(m):
        m["oh"].wait_recv()
        send(m["hy+"])
        send(m["hy-"])
        send(m["h0c"])

    def row_near(m, which):
        m[which + "y+"].wait_recv()
        send(m[which + "2y+"])
        send(m[which + "-c"])
        m[which + "y-"].wait_recv()
        send(m[which + "2y-"])
        send(m[which + "+c"])

    def row_far(m, which):
        m[which + "2y+"].wait_recv()
        m[which + "2y-"].wait_recv()
        send(m[which + "fc"])

    def row_finish(m):
        for name in m:
            if name.endswith("c"):
                m[name].wait_recv()

    loads[0].wait()
    row_start(cm)
    loads[1].wait()
    loads[2].wait()

    def activate(t, _):
        part = pl.ds(pl.multiple_of(t * 16, 16), 16)
        g = gate[part, :].astype(F32)
        u = up[part, :].astype(F32)
        s = 1.0 / (1.0 + jnp.exp(-g))
        sl = g * s
        silu[part, :] = sl
        slope[part, :] = u * s * (1.0 + g * (1.0 - s))
        gh_own[part, :] = sl * u
        return 0

    lax.fori_loop(0, TOK // 16, activate, 0)

    def turn(t, _):
        part = pl.ds(pl.multiple_of(t * 128, 128), 128)
        hid_t[part, toks(c)] = gh_own[:, part].T.astype(BF16)
        return 0

    lax.fori_loop(0, F // 128, turn, 0)

    def hid_add(name, c_, start, size, device):
        ref = hid_t.at[pl.ds(start, size), toks(c_)]
        hm[name] = message(HID0 + len(hm), ref, ref, device)

    hm = {}
    c_zp, c_zm, c_zf = xl * 4 + z_up, xl * 4 + z_dn, xl * 4 + z_far
    c_xzp, c_xzm, c_xzf = xo * 4 + z_up, xo * 4 + z_dn, xo * 4 + z_far
    A, B = F // 2, F // 4
    for way, device in (("z+", to_zp), ("z-", to_zm), ("x", to_xl)):
        hid_add("o0" + way, c, 0, A, device)
        hid_add("o1" + way, c, A, A, device)
    for way, near, xnear, at, device in (("z+", c_zm, c_xzm, 0, to_zp), ("z-", c_zp, c_xzp, B, to_zm)):
        hid_add("x0" + way, c_xl, 0, A, device)
        hid_add("f0" + way, near, at, B, device)
        hid_add("q0" + way, xnear, at, B, device)
        hid_add("f1" + way, near, A + at, B, device)
        hid_add("n1x" + way, near, A, A, to_xl)
    hid_add("zf1x", c_zf, A, A, to_xl)

    def hid_send(*names):
        for name in names:
            send(hm[name])

    def hid_wait(*names):
        for name in names:
            hm[name].wait_recv()

    hid_send("o1z+", "o1z-", "o0z+", "o0z-")

    loads[3].wait()

    def turn_inp(t, _):
        part = pl.ds(pl.multiple_of(t * 128, 128), 128)
        inp_t[part, rows(r)] = inp_own[:, part].astype(F32).T.astype(BF16)
        return 0

    lax.fori_loop(0, D // 128, turn_inp, 0)

    row_xh(cm)
    hid_send("o0x", "o1x")
    row_near(cm, "o")
    hid_wait("o1z+", "o1z-")
    hid_send("f1z+", "f1z-", "n1xz+", "n1xz-")
    row_near(cm, "h")
    hid_wait("o0x")
    hid_send("x0z+", "x0z-")
    hid_wait("o0z+", "o0z-")
    hid_send("f0z+", "f0z-")
    row_far(cm, "o")
    row_far(cm, "h")
    row_finish(cm)
    loads[4].wait()

    def gh_dot(c_):
        return lax.dot_general(cot[toks(c_), :], wd[...], ACROSS, preferred_element_type=F32)

    gm = {}

    def gh_add(name, i, device):
        gm[name] = message(GH0 + i, gh_send.at[i], gh_recv.at[i], device)

    for k, who in enumerate(("t", "o")):
        gh_add("r+" + who, 0 + k, to_zp)
        gh_add("r-" + who, 2 + k, to_zm)
        gh_add("d+" + who, 4 + k, to_zp)
        gh_add("d-" + who, 6 + k, to_zm)
        gh_add("k+" + who, 8 + k, to_zp)
        gh_add("k-" + who, 10 + k, to_zm)
        gh_add("x%d" % k, 12 + k, to_xl)
    sides = (("t", 0, xo), ("o", 1, xl))

    def gh_start(who, k, x_):
        part = gh_dot(x_ * 4 + z_far).astype(BF16)
        gh_send[0 + k] = part[:HALF]
        gh_send[2 + k] = part[HALF:]
        send(gm["r+" + who])
        send(gm["r-" + who])
        part = gh_dot(x_ * 4 + z_up)
        gh_send[4 + k] = part[HALF:].astype(BF16)
        gh_keep[k] = part[:HALF]
        send(gm["d+" + who])
        part = gh_dot(x_ * 4 + z_dn)
        gh_send[6 + k] = part[:HALF].astype(BF16)
        gh_keep[2 + k] = part[HALF:]
        send(gm["d-" + who])

    def gh_combine(who, k, x_):
        gm["r+" + who].wait_recv()
        gh_send[8 + k] = (gh_keep[k] + gh_recv[0 + k].astype(F32)).astype(BF16)
        send(gm["k+" + who])
        gm["r-" + who].wait_recv()
        gh_send[10 + k] = (gh_keep[2 + k] + gh_recv[2 + k].astype(F32)).astype(BF16)
        send(gm["k-" + who])

    gh_start(*sides[0])
    gh_own[...] = gh_dot(xo * 4 + z)
    row_start(im)
    gh_combine(*sides[0])
    gh_start(*sides[1])
    hid_wait("f1z+", "f1z-")
    hid_send("zf1x")
    row_xh(im)
    row_near(im, "o")
    gm["d+t"].wait_recv()
    gm["d-t"].wait_recv()
    gm["k+t"].wait_recv()
    gm["k-t"].wait_recv()
    gh_send[12] = (
        gh_own[pl.ds(0, HALF), :] + gh_recv[6].astype(F32) + gh_recv[8].astype(F32)
    ).astype(BF16)
    send(gm["x0"])
    gh_send[13] = (
        gh_own[pl.ds(HALF, HALF), :] + gh_recv[4].astype(F32) + gh_recv[10].astype(F32)
    ).astype(BF16)
    send(gm["x1"])
    gh_combine(*sides[1])
    hid_wait("x0z+", "x0z-")
    hid_send("q0z+", "q0z-")
    gh_own[...] = gh_dot(c)
    row_near(im, "h")
    gm["d+o"].wait_recv()
    gm["d-o"].wait_recv()
    gm["k+o"].wait_recv()
    gm["k-o"].wait_recv()

    gg = {}

    def g_add(name, c_, h, start, size, device):
        ref = grads.at[tile(c_ * TOK + h * HALF + start, size, 16), :]
        gg[name] = message(G0 + len(gg), ref, ref, device)

    across_x = HALF - FWD
    for h in (0, 1):
        for way, device in (("z+", to_zp), ("z-", to_zm), ("x", to_xl)):
            g_add("o%dz%s" % (h, way), c, h, 0, FWD, device)
            g_add("o%dx%s" % (h, way), c, h, FWD, across_x, device)
        g_add("x%dz+" % h, c_xl, h, FWD, across_x, to_zp)
        g_add("x%dz-" % h, c_xl, h, FWD, across_x, to_zm)
        g_add("zm%dx" % h, c_zm, h, 0, FWD, to_xl)
        g_add("zp%dx" % h, c_zp, h, 0, FWD, to_xl)
        g_add("zf%dx" % h, c_zf, h, 0, FWD, to_xl)
    for h, way, near, xnear, device in ((0, "z+", c_zm, c_xzm, to_zp), (1, "z-", c_zp, c_xzp, to_zm)):
        g_add("fz" + way, near, h, 0, FWD, device)
        g_add("fx" + way, near, h, FWD, across_x, device)
        g_add("q" + way, xnear, h, FWD, across_x - LATE, device)
        g_add("l" + way, xnear, h, HALF - LATE, LATE, device)

    for h in (0, 1):
        gm["x%d" % h].wait_recv()
        a, b = ((6, 8), (4, 10))[h]

        def grad(t, _, h=h, a=a, b=b):
            here = pl.ds(pl.multiple_of(t * 16, 16), 16)
            part = pl.ds(pl.multiple_of(h * HALF + t * 16, 16), 16)
            gh = (
                gh_own[part, :]
                + gh_recv[a + 1, here, :].astype(F32)
                + gh_recv[b + 1, here, :].astype(F32)
                + gh_recv[12 + h, here, :].astype(F32)
            )
            dst = tile(c * TOK + h * HALF + t * 16, 16, 16)
            grads[dst, pl.ds(0, F)] = (gh * slope[part, :]).astype(BF16)
            grads[dst, pl.ds(F, F)] = (gh * silu[part, :]).astype(BF16)
            return 0

        lax.fori_loop(0, HALF // 16, grad, 0)
        for part in "zx":
            for way in ("z+", "z-", "x"):
                send(gg["o%d%s%s" % (h, part, way)])

    loads[5].wait()
    loads[6].wait()

    pairs = []
    sums = []

    def gi_make(c_, start=0, size=HALF):
        i = len(pairs)
        spot = min(i, 7)
        both = jnp.concatenate(
            [grads[tile(c_ * TOK + h * HALF + start, size, 16), :] for h in (0, 1)], axis=0
        )
        gi_part[i % 2, pl.ds(0, 2 * size), :] = lax.dot_general(
            both, w_in[...], ACROSS, preferred_element_type=F32
        )
        here = pl.ds(start, size)
        theirs = tile((1 - core) * size, size, size)
        pair_send[spot, here, :] = gi_part[i % 2, theirs, :].astype(BF16)
        m = message(PAIR0 + i, pair_send.at[spot, here], pair_recv.at[spot, here], to_core)
        send(m)
        pairs.append((m, c_, start, size))

    def gi_sum():
        i = len(sums)
        spot = min(i, 7)
        m, c_, start, size = pairs[i]
        m.wait_recv()
        mine = tile(core * size, size, size)
        here = pl.ds(start, size)
        q_send[spot, here, :] = (
            gi_part[i % 2, mine, :] + pair_recv[spot, here, :].astype(F32)
        ).astype(BF16)
        y_, xh_ = lax.div(c_, 2), lax.rem(c_, 2)
        arrived = q_late_sem if i == 8 else q_recv_sem
        q = pltpu.make_async_remote_copy(
            src_ref=q_send.at[spot, here],
            dst_ref=q_recv.at[xh_ * 4 + y, here],
            send_sem=q_send_sem.at[i],
            recv_sem=arrived.at[xh_ * 4 + y],
            device_id=(row_of(y_, xh, core), c),
            device_id_type=MESH,
        )
        ours = y_ == y

        @pl.when(jnp.logical_not(ours))
        def _():
            q.start()

        @pl.when(ours)
        def _():
            q_recv[xh_ * 4 + y, here, :] = q_send[spot, here, :]

        sums.append((q, ours))

    def y_total(xh_, start, size, sem, store):
        here = pl.ds(start, size)
        for j in (1, 2, 3):
            slot = xh_ * 4 + lax.rem(y + j, 4)
            pltpu.make_async_remote_copy(
                src_ref=q_send.at[0, here],
                dst_ref=q_recv.at[slot, here],
                send_sem=q_send_sem.at[0],
                recv_sem=sem.at[slot],
                device_id=to_yp,
                device_id_type=MESH,
            ).wait_recv()

        def add(t, _):
            part = pl.ds(pl.multiple_of(start + t * 16, 16), 16)
            total = q_recv[xh_ * 4, part, :].astype(F32)
            for j in (1, 2, 3):
                total = total + q_recv[xh_ * 4 + j, part, :].astype(F32)
            store(part, total)
            return 0

        lax.fori_loop(0, size // 16, add, 0)

    last_xh = c_xzf == y * 2 + xho
    last_own = c_xzf == chip
    parts = (
        (jnp.logical_not(last_xh), 0, HALF, q_recv_sem),
        (last_xh, 0, HALF - LATE, q_recv_sem),
        (last_xh, HALF - LATE, LATE, q_late_sem),
    )
    fwd = []

    def forward(k):
        when, start, size, sem = parts[k]
        here = pl.ds(start, size)
        m = message(FWD0 + k, x_send.at[here], x_recv.at[here], to_xh)
        fwd.append(m)

        @pl.when(when)
        def _():
            def store(part, total):
                x_send[part, :] = total.astype(BF16)

            y_total(xho, start, size, sem, store)
            m.start()

    outs = []

    def down(t, _):
        part = pl.ds(pl.multiple_of(t * 224, 32), 224)
        dwd[part, :] = jnp.dot(
            hid_t[part, :], cot[...], preferred_element_type=F32
        ).astype(BF16)
        return 0

    gi_make(c)
    for name in ("o0zz+", "o0zz-"):
        gg[name].wait_recv()
    send(gg["fzz+"])
    send(gg["zm0x"])
    send(gg["zp0x"])
    hid_wait("f0z+", "f0z-", "q0z+", "q0z-")
    hid_wait("o1x", "n1xz+", "n1xz-", "zf1x")
    lax.fori_loop(0, 2, down, 0)
    row_far(im, "o")
    row_far(im, "h")
    gg["o0xz+"].wait_recv()
    send(gg["fxz+"])
    gg["o0xx"].wait_recv()
    send(gg["x0z+"])
    gg["o1zz+"].wait_recv()
    gg["o1zz-"].wait_recv()
    send(gg["fzz-"])
    send(gg["zm1x"])
    send(gg["zp1x"])
    lax.fori_loop(2, 4, down, 0)
    copy = pltpu.make_async_copy(dwd, dwd_hbm, out_sem.at[0])
    copy.start()
    outs.append(copy)
    gg["o1xz-"].wait_recv()
    send(gg["fxz-"])
    gg["o1xx"].wait_recv()
    send(gg["x1z-"])
    send(gg["x0z-"])
    send(gg["x1z+"])
    gg["fzz+"].wait_recv()
    send(gg["zf0x"])
    gg["fzz-"].wait_recv()
    send(gg["zf1x"])
    gg["o0zx"].wait_recv()
    gg["o1zx"].wait_recv()
    gi_make(c_xl)
    gi_sum()
    gg["o1xz+"].wait_recv()
    gi_make(c_zm)
    gi_sum()
    gg["o0xz-"].wait_recv()
    gi_make(c_zp)
    gi_sum()
    gg["fxz+"].wait_recv()
    gg["fxz-"].wait_recv()
    gi_make(c_zf)
    gi_sum()
    row_finish(im)

    def inward(t, _, x_, first):
        part = pl.ds(pl.multiple_of(t * 256, 256), 256)
        deep = tile(x_ * 1024, 1024, 1024)
        for k in (0, 1):
            part_sum = jnp.dot(
                inp_t[part, deep], grads[deep, pl.ds(k * F, F)], preferred_element_type=F32
            )
            if first:
                dw_sum[k, part, :] = part_sum
            else:
                dw[k, part, :] = (dw_sum[k, part, :] + part_sum).astype(BF16)
        return 0

    lax.fori_loop(0, 2, functools.partial(inward, x_=xl, first=True), 0)
    gg["x0z+"].wait_recv()
    send(gg["qz+"])
    send(gg["lz+"])
    gg["x1z-"].wait_recv()
    send(gg["qz-"])
    send(gg["lz-"])
    lax.fori_loop(2, 4, functools.partial(inward, x_=xl, first=True), 0)
    for h in (0, 1):
        gg["zm%dx" % h].wait_recv()
        gg["zp%dx" % h].wait_recv()
    gg["x1z+"].wait_recv()
    gi_make(c_xzm)
    gi_sum()
    gg["x0z-"].wait_recv()
    gi_make(c_xzp)
    gi_sum()
    for h in (0, 1):
        gg["zf%dx" % h].wait_recv()
    gg["qz+"].wait_recv()
    gg["qz-"].wait_recv()
    gi_make(c_xzf, 0, HALF - LATE)
    gi_sum()
    gg["lz+"].wait_recv()
    gg["lz-"].wait_recv()
    gi_make(c_xzf, HALF - LATE, LATE)
    gi_sum()
    gi_sum()
    forward(0)
    lax.fori_loop(0, 3, functools.partial(inward, x_=xo, first=False), 0)
    forward(1)
    lax.fori_loop(3, 4, functools.partial(inward, x_=xo, first=False), 0)
    forward(2)
    for k, dst in ((0, dwg_hbm), (1, dwu_hbm)):
        copy = pltpu.make_async_copy(dw.at[k], dst, out_sem.at[1 + k])
        copy.start()
        outs.append(copy)

    def finish(part, total):
        gi_out[part, :] = (total + x_recv[part, :].astype(F32)).astype(BF16)

    @pl.when(jnp.logical_not(last_own))
    def _():
        fwd[0].wait_recv()
        y_total(xh, 0, HALF, q_recv_sem, finish)

    @pl.when(last_own)
    def _():
        fwd[1].wait_recv()
        y_total(xh, 0, HALF - LATE, q_recv_sem, finish)
        fwd[2].wait_recv()
        y_total(xh, HALF - LATE, LATE, q_late_sem, finish)

    copy = pltpu.make_async_copy(gi_out, gi_hbm, out_sem.at[3])
    copy.start()
    outs.append(copy)
    for m in started:
        m.wait_send()
    for m, part in zip(fwd, parts):

        @pl.when(part[0])
        def _():
            m.wait_send()

    for q, ours in sums:

        @pl.when(jnp.logical_not(ours))
        def _():
            q.wait_send()

    for copy in outs:
        copy.wait()


def write_out(*refs):
    sources, targets, held = refs[:4], refs[4:8], refs[8:12]
    load_sem, store_sem = refs[12:]
    loads, stores = [], []
    for src, mid, dst in zip(sources, held, targets):
        step = src.shape[0] // PARTS
        for k in range(PARTS):
            here = pl.ds(k * step, step)
            i = len(loads)
            loads.append(pltpu.make_async_copy(src.at[here, :], mid.at[here, :], load_sem.at[i]))
            stores.append(pltpu.make_async_copy(mid.at[here, :], dst.at[here, :], store_sem.at[i]))
    for load in loads:
        load.start()
    for load, store in zip(loads, stores):
        load.wait()
        store.start()
    for store in stores:
        store.wait()


def shards(inputs, cotangent, gate_pre, up_pre, w_gate, w_up, w_down):
    anywhere = pl.BlockSpec(memory_space=pl.ANY)
    vmem = pltpu.VMEM
    dma = pltpu.SemaphoreType.DMA
    done = pl.pallas_call(
        kernel,
        out_shape=(
            jax.ShapeDtypeStruct((ROWS, D), BF16),
            jax.ShapeDtypeStruct((D, F), BF16),
            jax.ShapeDtypeStruct((D, F), BF16),
            jax.ShapeDtypeStruct((F, D), BF16),
        ),
        in_specs=[anywhere] * 7,
        out_specs=(anywhere,) * 4,
        scratch_shapes=[
            vmem((2048, D), BF16),
            vmem((D, 2048), BF16),
            vmem((F, 2048), BF16),
            vmem((2048, 2 * F), BF16),
            vmem((D, 2 * F), BF16),
            vmem((F, D), BF16),
            vmem((ROWS, D), BF16),
            vmem((TOK, F), BF16),
            vmem((TOK, F), BF16),
            vmem((TOK, F), F32),
            vmem((TOK, F), F32),
            vmem((14, HALF, F), BF16),
            vmem((14, HALF, F), BF16),
            vmem((4, HALF, F), F32),
            vmem((TOK, F), F32),
            vmem((2, TOK, D), F32),
            vmem((8, ROWS, D), BF16),
            vmem((8, ROWS, D), BF16),
            vmem((8, ROWS, D), BF16),
            vmem((8, ROWS, D), BF16),
            vmem((ROWS, D), BF16),
            vmem((ROWS, D), BF16),
            vmem((2, D, F), BF16),
            vmem((2, D, F), F32),
            vmem((F, D), BF16),
            vmem((ROWS, D), BF16),
            dma((N_SEM,)),
            dma((N_SEM,)),
            dma((9,)),
            dma((8,)),
            dma((8,)),
            dma((7,)),
            dma((4,)),
        ],
        compiler_params=pltpu.CompilerParams(
            collective_id=0, has_side_effects=True, vmem_limit_bytes=60 * 2**20
        ),
    )(inputs, cotangent, gate_pre, up_pre, w_gate, w_up, w_down)
    return pl.pallas_call(
        write_out,
        out_shape=tuple(jax.ShapeDtypeStruct(x.shape, BF16) for x in done),
        in_specs=[anywhere] * 4,
        out_specs=(anywhere,) * 4,
        scratch_shapes=[vmem(x.shape, BF16) for x in done] + [dma((4 * PARTS,))] * 2,
        compiler_params=pltpu.CompilerParams(vmem_limit_bytes=60 * 2**20),
    )(*done)


def solution(mesh):
    placed = (
        P("row", "col"),
        P("row", "col"),
        P("col", "row"),
        P("col", "row"),
        P("col", "row"),
        P("col", "row"),
        P("row", "col"),
    )
    return jax.shard_map(
        shards,
        mesh=mesh,
        in_specs=placed,
        out_specs=(P("row", "col"), P("col", "row"), P("col", "row"), P("row", "col")),
        check_vma=False,
    )
```

time: 162 us -> 149 us (0.920); the launches traced: 160 us -> 149 us
  local copies, waits for them, and re-layouts: 8.07 us -> 0 us
  Pallas kernels: 151 us -> 148 us
    unnamed x8 -> x0, local copies, waits for them, and re-layouts: 8.07 us -> none
    pallas_call x1, Pallas kernels: 151 us -> 143 us  [shards(): pl.pallas_call(kernel, out_shape=(jax.ShapeDtypeStruct((ROWS, D), BF16),...]
    pallas_call x0 -> x1, Pallas kernels: none -> 5.31 us  [shards(): pl.pallas_call(write_out, out_shape=tuple((jax.ShapeDtypeStruct(x.shape,...]
where the time goes in v2:
time: 149 us
  Pallas kernels  148 us (99%)
    pallas_call x1, Pallas kernels, shards(): pl.pallas_call(kernel, out_shape=(jax.ShapeDtypeStruct((ROWS, D), BF16),...  143 us
    pallas_call x1, Pallas kernels, shards(): pl.pallas_call(write_out, out_shape=tuple((jax.ShapeDtypeStruct(x.shape,...  5.31 us

profile of v2, /device:TPU:47, one launch (start us, length us, event | category | flops | bytes accessed | tf_op | source)
XLA Modules:
  0.0 149.0 jit_solution(2591924612474622548)
XLA Ops:
  0.6 142.9 %shard_map.102 = (bf16[128,1024]{1,0:T(8,128)(2,1)}, bf16[1024,896]{1,0:T(8,128)(2,1)}, bf16[1024,896]{1,0:T(8,128)(2,1)}, bf16[896,1024]{1,0:T(8,128)(2,1)}) custom-call(bf16[128,1024]{1,0:T(8,128)(2,1)} %inp_hbm.1, bf16[128,1024]{1,0:T(8,128)(2,1)} %cot_hbm.1, bf16[256,896]{1,0:T(8,128)(2,1)} %gate_hbm.1, bf16[256,896]{1,0:T(8,128)(2,1)} %up_hbm.1, ...), custom_call_target="tpu_custom_call" | custom-call | tf_op jit(solution)/shard_map/pallas_call | solution.py:664
  143.5 5.3 %shard_map.103 = (bf16[128,1024]{1,0:T(8,128)(2,1)}, bf16[1024,896]{1,0:T(8,128)(2,1)}, bf16[1024,896]{1,0:T(8,128)(2,1)}, bf16[896,1024]{1,0:T(8,128)(2,1)}) custom-call(bf16[128,1024]{1,0:T(8,128)(2,1)} %get-tuple-element.8.refs_0_, bf16[1024,896]{1,0:T(8,128)(2,1)} %get-tuple-element.9.refs_1_, bf16[1024,896]{1,0:T(8,128)(2,1)} %get-tuple-element.10.refs_2_, ...), custom_call_target="tpu_custom_call" | custom-call | tf_op jit(solution)/shard_map/pallas_call | solution.py:713

commit v3 on v2

--- a/solution.py
+++ b/solution.py
@@ -33,7 +33,7 @@
 N_FWD = 3
 FWD0 = PAIR0 + 9
 N_SEM = FWD0 + N_FWD
-PARTS = 4
+PARTS = 8
 
 
 def kernel(
@@ -586,10 +586,10 @@
     gg["qz-"].wait_recv()
     gi_make(c_xzf, 0, HALF - LATE)
     gi_sum()
+    gi_sum()
     gg["lz+"].wait_recv()
     gg["lz-"].wait_recv()
     gi_make(c_xzf, HALF - LATE, LATE)
-    gi_sum()
     gi_sum()
     forward(0)
     lax.fori_loop(0, 3, functools.partial(inward, x_=xo, first=False), 0)

time: 149 us -> 149 us (level)
  no operation moved by 1% of the time
where the time goes in v3:
time: 149 us
  Pallas kernels  148 us (99%)
    pallas_call x1, Pallas kernels, shards(): pl.pallas_call(kernel, out_shape=(jax.ShapeDtypeStruct((ROWS, D), BF16),...  143 us
    pallas_call x1, Pallas kernels, shards(): pl.pallas_call(write_out, out_shape=tuple((jax.ShapeDtypeStruct(x.shape,...  5.44 us

profile of v3, /device:TPU:47, one launch (start us, length us, event | category | flops | bytes accessed | tf_op | source)
XLA Modules:
  0.0 149.1 jit_solution(15394883078306988935)
XLA Ops:
  0.6 142.9 %shard_map.102 = (bf16[128,1024]{1,0:T(8,128)(2,1)}, bf16[1024,896]{1,0:T(8,128)(2,1)}, bf16[1024,896]{1,0:T(8,128)(2,1)}, bf16[896,1024]{1,0:T(8,128)(2,1)}) custom-call(bf16[128,1024]{1,0:T(8,128)(2,1)} %inp_hbm.1, bf16[128,1024]{1,0:T(8,128)(2,1)} %cot_hbm.1, bf16[256,896]{1,0:T(8,128)(2,1)} %gate_hbm.1, bf16[256,896]{1,0:T(8,128)(2,1)} %up_hbm.1, ...), custom_call_target="tpu_custom_call" | custom-call | tf_op jit(solution)/shard_map/pallas_call | solution.py:664
  143.5 5.4 %shard_map.103 = (bf16[128,1024]{1,0:T(8,128)(2,1)}, bf16[1024,896]{1,0:T(8,128)(2,1)}, bf16[1024,896]{1,0:T(8,128)(2,1)}, bf16[896,1024]{1,0:T(8,128)(2,1)}) custom-call(bf16[128,1024]{1,0:T(8,128)(2,1)} %get-tuple-element.8.refs_0_, bf16[1024,896]{1,0:T(8,128)(2,1)} %get-tuple-element.9.refs_1_, bf16[1024,896]{1,0:T(8,128)(2,1)} %get-tuple-element.10.refs_2_, ...), custom_call_target="tpu_custom_call" | custom-call | tf_op jit(solution)/shard_map/pallas_call | solution.py:713
